TPU v7x, 32 devices: a whole 2x2x4 slice. The times are simulated.
32 devices in a mesh: dp: 16 (over z, y, core), fsdp: 2 (over x).
Axes of the slice: x: 2, y: 2, z: 4, core: 2. Of those that a mesh axis runs over, the one named last changes fastest.
Arguments:
- inputs: bfloat16 [32768, 512], P(('dp', 'fsdp')), may hold values from -6 to 6
- documents: int32 [32, 1024], P(('dp', 'fsdp')), may hold values from 0 to 7, never falling along the last dimension, each value on 1 to 512 neighbouring positions
- first_gain: bfloat16 [512], P(('dp', 'fsdp')), may hold values from 0.5 to 1.5
- first_shift: bfloat16 [512], P(('dp', 'fsdp')), may hold values from -1.75 to 1.75
- attend_weight: bfloat16 [512, 1536], P(('dp', 'fsdp')), may hold values from -0.25 to 0.25
- position_table: bfloat16 [256], P(('dp', 'fsdp')), may hold values from -6 to 6
- output_weight: bfloat16 [512, 512], P(('dp', 'fsdp')), may hold values from -1.5 to 1.5
- output_shift: bfloat16 [512], P(('dp', 'fsdp')), may hold values from -1.75 to 1.75
- second_gain: bfloat16 [512], P(('dp', 'fsdp')), may hold values from 0.5 to 1.5
- second_shift: bfloat16 [512], P(('dp', 'fsdp')), may hold values from -1.75 to 1.75
- expand_weight: bfloat16 [512, 2048], P(('dp', 'fsdp')), may hold values from -0.25 to 0.25
- expand_shift: bfloat16 [2048], P(('dp', 'fsdp')), may hold values from -1.75 to 1.75
- reduce_weight: bfloat16 [2048, 512], P(('dp', 'fsdp')), may hold values from -0.125 to 0.125
- reduce_shift: bfloat16 [512], P(('dp', 'fsdp')), may hold values from -1.75 to 1.75
- cotangent: bfloat16 [32768, 512], P(('dp', 'fsdp')), may hold values from -6 to 6
Outputs:
- output: bfloat16 [32768, 512], P(('dp', 'fsdp'))
- input_grad: float32 [32768, 512], P(('dp', 'fsdp'))
- first_gain_grad: float32 [512], P(('dp', 'fsdp'))
- first_shift_grad: float32 [512], P(('dp', 'fsdp'))
- attend_weight_grad: float32 [512, 1536], P(('dp', 'fsdp'))
- position_table_grad: float32 [256], P(('dp', 'fsdp'))
- output_weight_grad: float32 [512, 512], P(('dp', 'fsdp'))
- output_shift_grad: float32 [512], P(('dp', 'fsdp'))
- second_gain_grad: float32 [512], P(('dp', 'fsdp'))
- second_shift_grad: float32 [512], P(('dp', 'fsdp'))
- expand_weight_grad: float32 [512, 2048], P(('dp', 'fsdp'))
- expand_shift_grad: float32 [2048], P(('dp', 'fsdp'))
- reduce_weight_grad: float32 [2048, 512], P(('dp', 'fsdp'))
- reduce_shift_grad: float32 [512], P(('dp', 'fsdp'))
Inputs may be any that keep to these rules, and one draw needn't show every extreme that they name: `documents`: in each row the document numbers never fall, every number up to 7 appears, no document has more than 512 tokens and one in each row has exactly that many.
All inputs are finite; a program needn't handle non-finite values.
Results may differ from a plain program's by a relative error of at most 0.02.
Values may be sent and summed in bfloat16 or wider, within the bound.
A program may use at most 256 MiB of HBM per device.

v0:
```python
import jax
import jax.numpy as jnp
from jax import lax
from jax.sharding import PartitionSpec as P

D = 512
HEADS = 8
HEAD_DIM = 64
BUCKETS = 32


eps = 1e-05
far_reach = 128


def bucket_of(distance):
    exact_count = BUCKETS // 2
    counted = jnp.minimum(distance, exact_count)
    for level_j in range(1, exact_count):
        border = int(exact_count * (far_reach / exact_count) ** (level_j / exact_count))
        counted = counted + (distance >= border).astype(jnp.int32)
    return counted


def normalize(values, norm_gain, norm_shift):
    center = values - jnp.mean(values, axis=-1, keepdims=True)
    spread = jnp.mean(center * center, axis=-1, keepdims=True)
    return center * lax.rsqrt(spread + eps) * norm_gain + norm_shift


def inner_rows(left_side, right_side):
    return lax.dot_general(
        left_side, right_side, (((0,), (0,)), ((), ())), preferred_element_type=jnp.float32
    )


def inner_cols(left_side, right_side):
    return lax.dot_general(
        left_side, right_side, (((1,), (1,)), ((), ())), preferred_element_type=jnp.float32
    )


def block_scores(block_q, key_heads, bias_table, doc_ids, first_row, block_rows):
    length = key_heads.shape[0]
    query_pos = first_row + lax.broadcasted_iota(jnp.int32, (block_rows, length), 0)
    key_pos = lax.broadcasted_iota(jnp.int32, (block_rows, length), 1)
    distance = query_pos - key_pos
    row_docs = lax.dynamic_slice_in_dim(doc_ids, first_row, block_rows)
    allowed = jnp.logical_and(distance >= 0, row_docs[:, None] == doc_ids[None, :])
    buckets = bucket_of(jnp.maximum(distance, 0)).reshape(1, block_rows * length)
    onehot = (buckets == lax.broadcasted_iota(jnp.int32, (BUCKETS, 1), 0)).astype(jnp.bfloat16)
    bias = jnp.dot(bias_table, onehot, preferred_element_type=jnp.float32).reshape(
        HEADS, block_rows, length
    )
    raw = jnp.einsum(
        "qhd,khd->hqk", block_q, key_heads, preferred_element_type=jnp.float32
    ) * HEAD_DIM ** (-0.5)
    return (jnp.where(allowed[None], raw + bias, -1e30), onehot)


def attention_forward(queries, key_heads, values, bias_table, doc_ids):
    length = queries.shape[0]
    block_rows = min(512, length)
    block_count = length // block_rows

    def one_block(block_index):
        first_row = block_index * block_rows
        block_q = lax.dynamic_slice_in_dim(queries, first_row, block_rows, 0)
        scores, onehot = block_scores(
            block_q, key_heads, bias_table, doc_ids, first_row, block_rows
        )
        row_peak = jnp.max(scores, axis=-1, keepdims=True)
        lifted = jnp.exp(scores - row_peak)
        totals = jnp.sum(lifted, axis=-1, keepdims=True)
        soft_weights = (lifted / totals).astype(jnp.bfloat16)
        attended = jnp.einsum(
            "hqk,khd->qhd", soft_weights, values, preferred_element_type=jnp.float32
        )
        return (attended.reshape(block_rows, D), (row_peak + jnp.log(totals))[..., 0])

    attended, logsum = lax.map(one_block, jnp.arange(block_count, dtype=jnp.int32))
    return (attended.reshape(length, D), logsum)


def attention_backward(queries, key_heads, values, bias_table, doc_ids, logsum, grad_attended):
    length = queries.shape[0]
    block_rows = min(512, length)
    block_count = length // block_rows
    scale_factor = HEAD_DIM ** (-0.5)

    def one_block(running, block_index):
        grad_keys, grad_values, grad_table = running
        first_row = block_index * block_rows
        block_q = lax.dynamic_slice_in_dim(queries, first_row, block_rows, 0)
        block_grad = lax.dynamic_slice_in_dim(grad_attended, first_row, block_rows, 0)
        scores, onehot = block_scores(
            block_q, key_heads, bias_table, doc_ids, first_row, block_rows
        )
        soft_weights = jnp.exp(scores - logsum[block_index][..., None])
        grad_soft = jnp.einsum(
            "qhd,khd->hqk", block_grad, values, preferred_element_type=jnp.float32
        )
        inner_sum = jnp.sum(soft_weights * grad_soft, axis=-1, keepdims=True)
        grad_scores = (soft_weights * (grad_soft - inner_sum)).astype(jnp.bfloat16)
        grad_table = grad_table + inner_cols(
            grad_scores.reshape(HEADS, block_rows * length), onehot
        )
        block_dq = (
            jnp.einsum("hqk,khd->qhd", grad_scores, key_heads, preferred_element_type=jnp.float32)
            * scale_factor
        )
        grad_keys = (
            grad_keys
            + jnp.einsum("hqk,qhd->khd", grad_scores, block_q, preferred_element_type=jnp.float32)
            * scale_factor
        )
        grad_values = grad_values + jnp.einsum(
            "hqk,qhd->khd",
            soft_weights.astype(jnp.bfloat16),
            block_grad,
            preferred_element_type=jnp.float32,
        )
        return ((grad_keys, grad_values, grad_table), block_dq)

    zeros_kv = jnp.zeros((length, HEADS, HEAD_DIM), jnp.float32)
    zeros_table = jnp.zeros((HEADS, BUCKETS), jnp.float32)
    (grad_keys, grad_values, grad_table), grad_queries = lax.scan(
        one_block, (zeros_kv, zeros_kv, zeros_table), jnp.arange(block_count, dtype=jnp.int32)
    )
    grad_projected = jnp.concatenate(
        [
            grad_queries.reshape(length, D),
            grad_keys.reshape(length, D),
            grad_values.reshape(length, D),
        ],
        axis=1,
    )
    return (grad_projected.astype(jnp.bfloat16), grad_table)


def attend_parts(layer_in, params, doc_ids):
    norm_gain, norm_shift, project_weight, bias_flat, out_weight, out_shift = params
    length = layer_in.shape[0]
    normed = normalize(
        layer_in, norm_gain.astype(jnp.float32), norm_shift.astype(jnp.float32)
    ).astype(jnp.bfloat16)
    projected = jnp.dot(normed, project_weight, preferred_element_type=jnp.float32).astype(
        jnp.bfloat16
    )
    projected = projected.reshape(length, 3, HEADS, HEAD_DIM)
    queries, key_heads, values = (projected[:, 0], projected[:, 1], projected[:, 2])
    bias_table = bias_flat.reshape(HEADS, BUCKETS)
    attended, logsum = attention_forward(queries, key_heads, values, bias_table, doc_ids)
    attended = attended.astype(jnp.bfloat16)
    branch = jnp.dot(attended, out_weight, preferred_element_type=jnp.float32) + out_shift.astype(
        jnp.float32
    )
    return (branch, (normed, queries, key_heads, values, bias_table, logsum, attended))


def feed_parts(residual, params):
    norm_gain, norm_shift, weight_in, shift_in, weight_out, shift_out = params
    normed = normalize(
        residual, norm_gain.astype(jnp.float32), norm_shift.astype(jnp.float32)
    ).astype(jnp.bfloat16)
    hidden = jnp.dot(normed, weight_in, preferred_element_type=jnp.float32) + shift_in.astype(
        jnp.float32
    )
    active = jax.nn.gelu(hidden, approximate=False).astype(jnp.bfloat16)
    branch = jnp.dot(active, weight_out, preferred_element_type=jnp.float32) + shift_out.astype(
        jnp.float32
    )
    return (branch, (normed, hidden, active))


def gelu_exact(values):
    return jax.nn.gelu(values, approximate=False)


def body(
    inputs,
    documents,
    first_gain,
    first_shift,
    attend_weight,
    position_table,
    output_weight,
    output_shift,
    second_gain,
    second_shift,
    expand_weight,
    expand_shift,
    reduce_weight,
    reduce_shift,
    cotangent,
):
    doc_ids = documents[0]
    attend_all = (
        lax.all_gather(first_gain, ("dp", "fsdp"), axis=0, tiled=True),
        lax.all_gather(first_shift, ("dp", "fsdp"), axis=0, tiled=True),
        lax.all_gather(attend_weight, ("dp", "fsdp"), axis=0, tiled=True),
        lax.all_gather(position_table, ("dp", "fsdp"), axis=0, tiled=True),
        lax.all_gather(output_weight, ("dp", "fsdp"), axis=0, tiled=True),
        lax.all_gather(output_shift, ("dp", "fsdp"), axis=0, tiled=True),
    )
    feed_all = (
        lax.all_gather(second_gain, ("dp", "fsdp"), axis=0, tiled=True),
        lax.all_gather(second_shift, ("dp", "fsdp"), axis=0, tiled=True),
        lax.all_gather(expand_weight, ("dp", "fsdp"), axis=0, tiled=True),
        lax.all_gather(expand_shift, ("dp", "fsdp"), axis=0, tiled=True),
        lax.all_gather(reduce_weight, ("dp", "fsdp"), axis=0, tiled=True),
        lax.all_gather(reduce_shift, ("dp", "fsdp"), axis=0, tiled=True),
    )
    layer_in = inputs.astype(jnp.float32)
    attend_out, unused_a = attend_parts(layer_in, attend_all, doc_ids)
    residual = layer_in + attend_out
    feed_out, unused_f = feed_parts(residual, feed_all)
    output = (residual + feed_out).astype(jnp.bfloat16)
    feed_back = (
        lax.all_gather(second_gain, ("dp", "fsdp"), axis=0, tiled=True),
        lax.all_gather(second_shift, ("dp", "fsdp"), axis=0, tiled=True),
        lax.all_gather(expand_weight, ("dp", "fsdp"), axis=0, tiled=True),
        lax.all_gather(expand_shift, ("dp", "fsdp"), axis=0, tiled=True),
        lax.all_gather(reduce_weight, ("dp", "fsdp"), axis=0, tiled=True),
        lax.all_gather(reduce_shift, ("dp", "fsdp"), axis=0, tiled=True),
    )
    attend_back = (
        lax.all_gather(first_gain, ("dp", "fsdp"), axis=0, tiled=True),
        lax.all_gather(first_shift, ("dp", "fsdp"), axis=0, tiled=True),
        lax.all_gather(attend_weight, ("dp", "fsdp"), axis=0, tiled=True),
        lax.all_gather(position_table, ("dp", "fsdp"), axis=0, tiled=True),
        lax.all_gather(output_weight, ("dp", "fsdp"), axis=0, tiled=True),
        lax.all_gather(output_shift, ("dp", "fsdp"), axis=0, tiled=True),
    )
    upstream = cotangent.astype(jnp.float32)
    unused_b, (normed_f, hidden, active) = feed_parts(residual, feed_back)
    reduce_w_grad = inner_rows(active, cotangent)
    reduce_b_grad = jnp.sum(cotangent.astype(jnp.float32), axis=0)
    grad_active = inner_cols(cotangent, feed_back[4])
    unused_g, gelu_pull = jax.vjp(gelu_exact, hidden)
    grad_hidden = gelu_pull(grad_active)[0].astype(jnp.bfloat16)
    expand_w_grad = inner_rows(normed_f, grad_hidden)
    expand_b_grad = jnp.sum(grad_hidden.astype(jnp.float32), axis=0)
    grad_normed_f = inner_cols(grad_hidden, feed_back[2])
    unused_n, norm_pull = jax.vjp(
        normalize, residual, feed_back[0].astype(jnp.float32), feed_back[1].astype(jnp.float32)
    )
    grad_res_norm, second_g_grad, second_s_grad = norm_pull(grad_normed_f)
    grad_residual = upstream + grad_res_norm
    feed_grads = (
        lax.psum_scatter(second_g_grad, ("dp", "fsdp"), scatter_dimension=0, tiled=True),
        lax.psum_scatter(second_s_grad, ("dp", "fsdp"), scatter_dimension=0, tiled=True),
        lax.psum_scatter(expand_w_grad, ("dp", "fsdp"), scatter_dimension=0, tiled=True),
        lax.psum_scatter(expand_b_grad, ("dp", "fsdp"), scatter_dimension=0, tiled=True),
        lax.psum_scatter(reduce_w_grad, ("dp", "fsdp"), scatter_dimension=0, tiled=True),
        lax.psum_scatter(reduce_b_grad, ("dp", "fsdp"), scatter_dimension=0, tiled=True),
    )
    unused_c, (normed_a, queries, key_heads, values, bias_table, logsum, attended) = attend_parts(
        layer_in, attend_back, doc_ids
    )
    grad_branch = grad_residual.astype(jnp.bfloat16)
    output_w_grad = inner_rows(attended, grad_branch)
    output_b_grad = jnp.sum(grad_branch.astype(jnp.float32), axis=0)
    length = layer_in.shape[0]
    grad_attended = (
        inner_cols(grad_branch, attend_back[4])
        .astype(jnp.bfloat16)
        .reshape(length, HEADS, HEAD_DIM)
    )
    grad_projected, grad_table = attention_backward(
        queries, key_heads, values, bias_table, doc_ids, logsum, grad_attended
    )
    attend_w_grad = inner_rows(normed_a, grad_projected)
    grad_normed_a = inner_cols(grad_projected, attend_back[2])
    unused_m, first_pull = jax.vjp(
        normalize, layer_in, attend_back[0].astype(jnp.float32), attend_back[1].astype(jnp.float32)
    )
    grad_in_norm, first_g_grad, first_s_grad = first_pull(grad_normed_a)
    input_grad = grad_residual + grad_in_norm
    table_flat = grad_table.reshape(HEADS * BUCKETS)
    attend_grads = (
        lax.psum_scatter(first_g_grad, ("dp", "fsdp"), scatter_dimension=0, tiled=True),
        lax.psum_scatter(first_s_grad, ("dp", "fsdp"), scatter_dimension=0, tiled=True),
        lax.psum_scatter(attend_w_grad, ("dp", "fsdp"), scatter_dimension=0, tiled=True),
        lax.psum_scatter(table_flat, ("dp", "fsdp"), scatter_dimension=0, tiled=True),
        lax.psum_scatter(output_w_grad, ("dp", "fsdp"), scatter_dimension=0, tiled=True),
        lax.psum_scatter(output_b_grad, ("dp", "fsdp"), scatter_dimension=0, tiled=True),
    )
    return (
        output,
        input_grad,
        attend_grads[0],
        attend_grads[1],
        attend_grads[2],
        attend_grads[3],
        attend_grads[4],
        attend_grads[5],
        feed_grads[0],
        feed_grads[1],
        feed_grads[2],
        feed_grads[3],
        feed_grads[4],
        feed_grads[5],
    )


def solution(mesh):
    placed = (
        P(("dp", "fsdp"), None),
        P(("dp", "fsdp"), None),
        P(("dp", "fsdp")),
        P(("dp", "fsdp")),
        P(("dp", "fsdp"), None),
        P(("dp", "fsdp")),
        P(("dp", "fsdp"), None),
        P(("dp", "fsdp")),
        P(("dp", "fsdp")),
        P(("dp", "fsdp")),
        P(("dp", "fsdp"), None),
        P(("dp", "fsdp")),
        P(("dp", "fsdp"), None),
        P(("dp", "fsdp")),
        P(("dp", "fsdp"), None),
    )
    return jax.shard_map(
        body,
        mesh=mesh,
        in_specs=placed,
        out_specs=(
            P(("dp", "fsdp"), None),
            P(("dp", "fsdp"), None),
            P(("dp", "fsdp")),
            P(("dp", "fsdp")),
            P(("dp", "fsdp"), None),
            P(("dp", "fsdp")),
            P(("dp", "fsdp"), None),
            P(("dp", "fsdp")),
            P(("dp", "fsdp")),
            P(("dp", "fsdp")),
            P(("dp", "fsdp"), None),
            P(("dp", "fsdp")),
            P(("dp", "fsdp"), None),
            P(("dp", "fsdp")),
        ),
        check_vma=False,
    )
```

profile of v0, /device:TPU:0, one launch (start us, length us, event | category | flops | bytes accessed | tf_op | source)
XLA Modules:
  0.0 1176.8 jit_solution(14121104356216622683)
XLA Ops:
  16.3 42.2 %all-reduce.17 = (bf16[512]{0:T(512)(128)(2,1)S(1)}, bf16[512]{0:T(512)(128)(2,1)S(1)}, bf16[256]{0:T(256)(128)(2,1)S(1)}, bf16[512]{0:T(512)(128)(2,1)S(1)}, bf...) all-reduce(bf16[512]{0:T(512)(128)(2,1)S(1)} %dynamic-update-slice., ...), channel_id=1, replica_groups=mesh['dp'=16,'fsdp'=2] {'dp','fsdp'}, use_global_device_ids=true, to_apply=%add.1 | all-reduce | flops 5376 | bytes 21504
  60.9 75.0 %all_gather.50 = bf16[512,512]{1,0:T(8,128)(2,1)} all-gather(bf16[16,512]{1,0:T(8,128)(2,1)} %param.27), channel_id=1, replica_groups=mesh['dp'=16,'fsdp'=2] {'dp','fsdp'}, dimensions={0}, use_global_device_ids=true | all-gather | bytes 540672 | tf_op jit(solution)/shard_map/all_gather | solution.py:203
  152.5 136.9 %while.40 = (s32[]{:T(128)}, bf16[2,512,512]{2,1,0:T(8,128)(2,1)}, f32[2,8,512]{2,1,0:T(8,128)S(1)}, s32[2]{0:T(128)S(1)}, s32[1024]{0:T(1024)S(1)}, /*index=5*/...) while((s32[]{:T(128)}, bf16[2,512,512]{2,1,0:T(8,128)(2,1)}, ...), condition=%wide.region_13.14_spmd, body=%wide.region_10.13_spmd.sunk | while | flops 1424486912 | bytes 203571968 | solution.py:81
  174.5 12.8 %fusion.214 = f32[524288,8]{0,1:T(8,128)} fusion(bf16[8,32]{1,0:T(8,128)(2,1)S(1)} %get-tuple-element.722, s32[524288]{0:T(1024)S(1)} %add_add_fusion.11), kind=kOutput, calls=%fused_computation.40.clone.1 | convolution fusion | flops 285212672 | bytes 18874880 | tf_op jit(solution)/shard_map/while/body/eval_jaxpr/dot_general | solution.py:52
  187.4 21.4 %fusion.215 = (f32[8,512]{1,0:T(8,128)S(1)}, f32[8,512,1024]{2,1,0:T(8,128)}) fusion(f32[1,8,512,1024]{3,1,2,0:T(8,128)} %bitcast.251, bf16[1024,8,64]{0,2,1:T(8,128)(2,1)S(1)} %get-tuple-element.721, bf16[1024,8,64]{0,2,1:T(8,128)(2,1)S(1)} %get-tuple-element.720, s32[]{:T(128)S(6)} %select_n.43, pred[512,1024]{1,0:T(8,128)(4,1)S(1)} %get-tuple-element.623), kind=kOutput, calls=%fused_computation.202.clone.1 | convolution fusion | flops 553644032 | bytes 35667972 | tf_op jit(solution)/shard_map/while/body/eval_jaxpr/qhd,khd->hqk/dot_general | solution.py:55
  236.1 12.8 %fusion.214 = f32[524288,8]{0,1:T(8,128)} fusion(bf16[8,32]{1,0:T(8,128)(2,1)S(1)} %get-tuple-element.722, s32[524288]{0:T(1024)S(1)} %add_add_fusion.11), kind=kOutput, calls=%fused_computation.40.clone.1 | convolution fusion | flops 285212672 | bytes 18874880 | tf_op jit(solution)/shard_map/while/body/eval_jaxpr/dot_general | solution.py:52
  249.0 21.4 %fusion.215 = (f32[8,512]{1,0:T(8,128)S(1)}, f32[8,512,1024]{2,1,0:T(8,128)}) fusion(f32[1,8,512,1024]{3,1,2,0:T(8,128)} %bitcast.251, bf16[1024,8,64]{0,2,1:T(8,128)(2,1)S(1)} %get-tuple-element.721, bf16[1024,8,64]{0,2,1:T(8,128)(2,1)S(1)} %get-tuple-element.720, s32[]{:T(128)S(6)} %select_n.43, pred[512,1024]{1,0:T(8,128)(4,1)S(1)} %get-tuple-element.623), kind=kOutput, calls=%fused_computation.202.clone.1 | convolution fusion | flops 553644032 | bytes 35667972 | tf_op jit(solution)/shard_map/while/body/eval_jaxpr/qhd,khd->hqk/dot_general | solution.py:55
  290.5 174.0 %while.39 = (s32[]{:T(128)}, bf16[2,512,512]{2,1,0:T(8,128)(2,1)}, s32[2]{0:T(128)S(1)}, s32[1024]{0:T(1024)S(1)}, s32[1,1024]{1,0:T(1,128)S(1)}, /*index=5*/bf1...) while((s32[]{:T(128)}, bf16[2,512,512]{2,1,0:T(8,128)(2,1)}, ...), condition=%wide.region_5.6_spmd, body=%wide.region_2.5_spmd.sunk | while | flops 1420302848 | bytes 136364752 | solution.py:81
  314.4 12.8 %fusion.206 = f32[524288,8]{0,1:T(8,128)} fusion(bf16[8,32]{1,0:T(8,128)(2,1)S(1)} %get-tuple-element.680, s32[524288]{0:T(1024)S(1)} %add_add_fusion.10), kind=kOutput, calls=%fused_computation.2.clone.1 | convolution fusion | flops 285212672 | bytes 18874880 | tf_op jit(solution)/shard_map/while/body/eval_jaxpr/dot_general | solution.py:52
  327.3 20.9 %fusion.207 = f32[8,512,1024]{2,1,0:T(8,128)} fusion(f32[1,8,512,1024]{3,1,2,0:T(8,128)} %bitcast.253, bf16[1024,8,64]{0,2,1:T(8,128)(2,1)S(1)} %get-tuple-element.679, pred[512,1024]{1,0:T(8,128)(4,1)S(1)} %get-tuple-element.608, bf16[1024,8,64]{0,2,1:T(8,128)(2,1)S(1)} %get-tuple-element.678, s32[]{:T(128)S(6)} %select_n.42), kind=kOutput, calls=%fused_computation.5.clone.1 | convolution fusion | flops 549453824 | bytes 35651588 | tf_op jit(solution)/shard_map/while/body/eval_jaxpr/qhd,khd->hqk/dot_general | solution.py:55
  348.1 13.8 %fusion.208 = f32[8,512]{1,0:T(8,128)S(1)} fusion(f32[8,512,1024]{2,1,0:T(8,128)} %fusion.207), kind=kOutput, calls=%fused_computation.201.clone.1 | output fusion | flops 8389631 | bytes 16793600 | tf_op jit(solution)/shard_map/while/body/eval_jaxpr/sub | solution.py:73
  361.9 19.2 %fusion.209 = bf16[8,512,64]{1,2,0:T(8,128)(2,1)} fusion(bf16[1024,8,64]{0,2,1:T(8,128)(2,1)S(1)} %get-tuple-element.681, f32[8,512]{1,0:T(8,128)S(1)} %fusion.208, f32[8,512,1024]{2,1,0:T(8,128)} %fusion.207), kind=kOutput, calls=%fused_computation.8.clone.1 | convolution fusion | flops 549458944 | bytes 18366464 | tf_op jit(solution)/shard_map/while/body/eval_jaxpr/hqk,khd->qhd/dot_general | solution.py:76
  393.4 12.8 %fusion.206 = f32[524288,8]{0,1:T(8,128)} fusion(bf16[8,32]{1,0:T(8,128)(2,1)S(1)} %get-tuple-element.680, s32[524288]{0:T(1024)S(1)} %add_add_fusion.10), kind=kOutput, calls=%fused_computation.2.clone.1 | convolution fusion | flops 285212672 | bytes 18874880 | tf_op jit(solution)/shard_map/while/body/eval_jaxpr/dot_general | solution.py:52
  406.3 20.9 %fusion.207 = f32[8,512,1024]{2,1,0:T(8,128)} fusion(f32[1,8,512,1024]{3,1,2,0:T(8,128)} %bitcast.253, bf16[1024,8,64]{0,2,1:T(8,128)(2,1)S(1)} %get-tuple-element.679, pred[512,1024]{1,0:T(8,128)(4,1)S(1)} %get-tuple-element.608, bf16[1024,8,64]{0,2,1:T(8,128)(2,1)S(1)} %get-tuple-element.678, s32[]{:T(128)S(6)} %select_n.42), kind=kOutput, calls=%fused_computation.5.clone.1 | convolution fusion | flops 549453824 | bytes 35651588 | tf_op jit(solution)/shard_map/while/body/eval_jaxpr/qhd,khd->hqk/dot_general | solution.py:55
  427.2 13.8 %fusion.208 = f32[8,512]{1,0:T(8,128)S(1)} fusion(f32[8,512,1024]{2,1,0:T(8,128)} %fusion.207), kind=kOutput, calls=%fused_computation.201.clone.1 | output fusion | flops 8389631 | bytes 16793600 | tf_op jit(solution)/shard_map/while/body/eval_jaxpr/sub | solution.py:73
  441.0 19.2 %fusion.209 = bf16[8,512,64]{1,2,0:T(8,128)(2,1)} fusion(bf16[1024,8,64]{0,2,1:T(8,128)(2,1)S(1)} %get-tuple-element.681, f32[8,512]{1,0:T(8,128)S(1)} %fusion.208, f32[8,512,1024]{2,1,0:T(8,128)} %fusion.207), kind=kOutput, calls=%fused_computation.8.clone.1 | convolution fusion | flops 549458944 | bytes 18366464 | tf_op jit(solution)/shard_map/while/body/eval_jaxpr/hqk,khd->qhd/dot_general | solution.py:76
  468.7 24.5 %multiply_convert_fusion.1 = (bf16[1024,2048]{1,0:T(8,128)(2,1)}, f32[1024,2048]{1,0:T(8,128)}, f32[1024,2048]{1,0:T(8,128)}) fusion(f32[2048]{0:T(1024)S(1)} %copy-done.58, bf16[512,2048]{1,0:T(8,128)(2,1)} %all-gather.6.cloned.1.call-done, f32[1024,512]{0,1:T(8,128)} %copy-done.20, f32[512]{0:T(512)S(1)} %copy-done.61, f32[512]{0:T(512)S(1)} %copy-done.54, ...), kind=kOutput, calls=%fused_computation.137 | convolution fusion | flops 2288517120 | bytes 25186304 | tf_op jit(solution)/shard_map/dot_general | solution.py:166
  521.1 255.6 %while.41 = (s32[]{:T(128)}, f32[1024,8,64]{0,2,1:T(8,128)}, f32[1024,8,64]{0,2,1:T(8,128)}, f32[8,32]{1,0:T(8,128)S(1)}, bf16[2,512,8,64]{1,3,2,0:T(8,128)(2,1)...) while((s32[]{:T(128)}, f32[1024,8,64]{0,2,1:T(8,128)}, ...), condition=%wide.region_16.17_spmd.clone, body=%wide.region_14.16_spmd.clone.sunk | while | flops 3327390720 | bytes 366054656 | solution.py:127
  563.6 12.8 %fusion.231 = f32[524288,8]{0,1:T(8,128)} fusion(bf16[8,32]{1,0:T(8,128)(2,1)S(1)} %get-tuple-element.776, s32[524288]{0:T(1024)S(1)} %add_add_fusion.12), kind=kOutput, calls=%fused_computation.80.clone.1 | convolution fusion | flops 285212672 | bytes 18874880 | tf_op jit(solution)/shard_map/while/body/eval_jaxpr/dot_general | solution.py:52
  576.4 25.4 %multiply_reduce_fusion.5 = (f32[8,512]{1,0:T(8,128)S(1)}, f32[8,512,1024]{2,1,0:T(8,128)}) fusion(f32[8,512,1024]{2,1,0:T(8,128)} %fusion.229, f32[8,512]{1,0:T(8,128)S(1)} %dynamic-slice_bitcast_fusion.2, f32[1,8,512,1024]{3,1,2,0:T(8,128)} %bitcast.252, bf16[1024,8,64]{0,2,1:T(8,128)(2,1)S(1)} %get-tuple-element.775, ...), kind=kOutput, calls=%fused_computation.88.clone.1 | convolution fusion | flops 562032640 | bytes 52461572 | tf_op jit(solution)/shard_map/while/body/eval_jaxpr/qhd,khd->hqk/dot_general | solution.py:55
  601.8 11.6 multiply_convert_fusion.3
  632.0 12.2 %copy.147 = bf16[1,8,512,1024]{3,1,2,0:T(8,128)(2,1)} copy(bf16[1,8,512,1024]{3,2,1,0:T(8,128)(2,1)} %bitcast.250) | data formatting | bytes 16777216 | tf_op jit(solution)/shard_map/while
  644.2 12.9 %fusion.232 = f32[8,32]{1,0:T(8,128)S(1)} fusion(bf16[8,524288]{1,0:T(8,128)(2,1)} %bitcast.254, s32[524288]{0:T(1024)S(1)} %copy-done.3, f32[8,32]{1,0:T(8,128)S(1)} %get-tuple-element.750, pred[]{:T(512)S(6)} %compare.3), kind=kOutput, calls=%fused_computation.121.clone.1 | convolution fusion | flops 285213184 | bytes 10487809 | tf_op jit(solution)/shard_map/while/body/eval_jaxpr/dot_general | solution.py:38
  676.2 12.8 %fusion.231 = f32[524288,8]{0,1:T(8,128)} fusion(bf16[8,32]{1,0:T(8,128)(2,1)S(1)} %get-tuple-element.776, s32[524288]{0:T(1024)S(1)} %add_add_fusion.12), kind=kOutput, calls=%fused_computation.80.clone.1 | convolution fusion | flops 285212672 | bytes 18874880 | tf_op jit(solution)/shard_map/while/body/eval_jaxpr/dot_general | solution.py:52
  689.0 25.3 %multiply_reduce_fusion.5 = (f32[8,512]{1,0:T(8,128)S(1)}, f32[8,512,1024]{2,1,0:T(8,128)}) fusion(f32[8,512,1024]{2,1,0:T(8,128)} %fusion.229, f32[8,512]{1,0:T(8,128)S(1)} %dynamic-slice_bitcast_fusion.2, f32[1,8,512,1024]{3,1,2,0:T(8,128)} %bitcast.252, bf16[1024,8,64]{0,2,1:T(8,128)(2,1)S(1)} %get-tuple-element.775, ...), kind=kOutput, calls=%fused_computation.88.clone.1 | convolution fusion | flops 562032640 | bytes 52461572 | tf_op jit(solution)/shard_map/while/body/eval_jaxpr/qhd,khd->hqk/dot_general | solution.py:55
  714.3 11.5 multiply_convert_fusion.3
  744.4 12.2 %copy.147 = bf16[1,8,512,1024]{3,1,2,0:T(8,128)(2,1)} copy(bf16[1,8,512,1024]{3,2,1,0:T(8,128)(2,1)} %bitcast.250) | data formatting | bytes 16777216 | tf_op jit(solution)/shard_map/while
  756.6 12.9 %fusion.232 = f32[8,32]{1,0:T(8,128)S(1)} fusion(bf16[8,524288]{1,0:T(8,128)(2,1)} %bitcast.254, s32[524288]{0:T(1024)S(1)} %copy-done.3, f32[8,32]{1,0:T(8,128)S(1)} %get-tuple-element.750, pred[]{:T(512)S(6)} %compare.3), kind=kOutput, calls=%fused_computation.121.clone.1 | convolution fusion | flops 285213184 | bytes 10487809 | tf_op jit(solution)/shard_map/while/body/eval_jaxpr/dot_general | solution.py:38
  824.3 38.0 %all-reduce.16 = (f32[512]{0:T(512)S(1)}, f32[512]{0:T(512)S(1)}, f32[256]{0:T(256)S(1)}, f32[512]{0:T(512)S(1)}, f32[512]{0:T(512)S(1)}, /*index=5*/f32[512]{0:T(512)S(1)}, f32[2048]{0:T(1024)S(1)}, f32[512]{0:T(512)S(1)}) all-reduce(f32[512]{0:T(512)S(1)} %get-tuple-element.285, ...), channel_id=2, replica_groups=mesh['dp'=16,'fsdp'=2] {'dp','fsdp'}, use_global_device_ids=true, to_apply=%region_20.21.clone | all-reduce | flops 5376 | bytes 43008
  869.9 14.5 %reduce-scatter.5.cloned.1.call-done = f32[16,1536]{1,0:T(8,128)} async-done(((f32[512,1536]{1,0:T(8,128)}), f32[16,1536]{1,0:T(8,128)}) %reduce-scatter.5.cloned.1.call-update) | async-done | bytes 98320 | tf_op jit(solution)/shard_map/reduce_scatter | solution.py:284
  884.3 143.8 %reduce-scatter.11.cloned.1.call-done = f32[64,512]{1,0:T(8,128)} async-done(((f32[2048,512]{1,0:T(8,128)}), f32[64,512]{1,0:T(8,128)}) %reduce-scatter.11.cloned.1.call-update) | async-done | bytes 131088 | tf_op jit(solution)/shard_map/reduce_scatter | solution.py:255
  1028.2 141.5 %reduce-scatter.9.cloned.1.call-done = f32[16,2048]{1,0:T(8,128)} async-done(((f32[512,2048]{1,0:T(8,128)}), f32[16,2048]{1,0:T(8,128)}) %reduce-scatter.9.cloned.1.call-update) | async-done | bytes 131088 | tf_op jit(solution)/shard_map/reduce_scatter | solution.py:253
  (363 shorter events, 262.0 us)
Async XLA Ops:
  7.2 132.2 %all-gather.4.cloned.1.call-start = ((), (), s32[]{:S(2)}) async-start(), calls=%async_computation.4 | async-start | bytes 1622016 | tf_op jit(solution)/shard_map/all_gather | solution.py:201
  7.9 460.7 %all-gather.6.cloned.1.call-start = ((), (), s32[]{:S(2)}) async-start(), calls=%async_computation.5 | async-start | bytes 2162688 | tf_op jit(solution)/shard_map/all_gather | solution.py:209
  8.7 484.5 %all-gather.8.cloned.1.call-start = ((), (), s32[]{:S(2)}) async-start(), calls=%async_computation.6 | async-start | bytes 2162688 | tf_op jit(solution)/shard_map/all_gather | solution.py:211
  9.4 860.5 %reduce-scatter.7.cloned.1.call-start = ((), (), s32[]{:S(2)}) async-start(), calls=%async_computation.8 | async-start | bytes 1081344 | tf_op jit(solution)/shard_map/reduce_scatter | solution.py:286
  58.5 80.8 %copy-start.63 = (f32[512]{0:T(512)}, f32[512]{0:T(512)S(1)}, u32[]{:S(2)}) copy-start(f32[512]{0:T(512)S(1)} %convert_element_type.549) | copy-start | bytes 6148
  58.5 80.8 %copy-start.52 = (f32[512]{0:T(512)}, f32[512]{0:T(512)S(1)}, u32[]{:S(2)}) copy-start(f32[512]{0:T(512)S(1)} %convert_element_type.548) | copy-start | bytes 6148
  208.8 10.6 copy-start.1
  270.4 10.6 copy-start.1
  290.4 174.0 %copy-start.65 = (f32[512]{0:T(512)S(1)}, f32[512]{0:T(512)}, u32[]{:S(2)}) copy-start(f32[512]{0:T(512)} %convert_element_type.554) | copy-start | bytes 6148
  467.0 48.1 %copy-start.42 = (f32[1024]{0:T(1024)}, f32[1024]{0:T(1024)S(1)}, u32[]{:S(2)}) copy-start(f32[1024]{0:T(1024)S(1)} %broadcast_multiply_fusion) | copy-start | bytes 12292
  468.6 46.6 %copy-start.50 = (f32[1024]{0:T(1024)}, f32[1024]{0:T(1024)S(1)}, u32[]{:S(2)}) copy-start(f32[1024]{0:T(1024)S(1)} %fusion.114) | copy-start | bytes 12292
  493.2 11.1 copy-start.68
  521.0 363.3 %reduce-scatter.5.cloned.1.call-start = ((), (), s32[]{:S(2)}) async-start(), calls=%async_computation.7 | async-start | bytes 3244032 | tf_op jit(solution)/shard_map/reduce_scatter | solution.py:284
  544.5 10.2 copy-start.9
  601.8 11.6 copy-start.11
  601.8 11.6 copy-start.17
  613.4 14.8 %copy-start = (bf16[8,512,1024]{2,1,0:T(8,128)(2,1)}, bf16[8,512,1024]{2,1,0:T(8,128)(2,1)S(1)}, u32[]{:S(2)}) copy-start(bf16[8,512,1024]{2,1,0:T(8,128)(2,1)S(1)} %multiply_convert_fusion.3) | copy-start | bytes 25165828 | tf_op jit(solution)/shard_map/while
  613.4 12.1 %copy-start.33 = (bf16[2,512,8,64]{1,3,2,0:T(8,128)(2,1)S(1)}, bf16[2,512,8,64]{1,3,2,0:T(8,128)(2,1)}, u32[]{:S(2)}) copy-start(bf16[2,512,8,64]{1,3,2,0:T(8,128)(2,1)} %get-tuple-element.751) | copy-start | bytes 3145732 | tf_op jit(solution)/shard_map/while
  632.0 12.2 %copy-start.5 = (f32[1024,8,64]{0,2,1:T(8,128)}, f32[1024,8,64]{0,2,1:T(8,128)S(1)}, u32[]{:S(2)}) copy-start(f32[1024,8,64]{0,2,1:T(8,128)S(1)} %bitcast_add_fusion.7) | copy-start | bytes 6291460 | tf_op jit(solution)/shard_map/while
  632.0 12.2 %copy-start.3 = (s32[524288]{0:T(1024)S(1)}, s32[524288]{0:T(1024)}, u32[]{:S(2)}) copy-start(s32[524288]{0:T(1024)} %copy-done.2) | copy-start | bytes 6291460 | tf_op jit(solution)/shard_map/while
  644.2 12.9 %copy-start.8 = (bf16[1024,8,64]{0,2,1:T(8,128)(2,1)S(1)}, bf16[1024,8,64]{0,2,1:T(8,128)(2,1)}, u32[]{:S(2)}) copy-start(bf16[1024,8,64]{0,2,1:T(8,128)(2,1)} %copy-done.7) | copy-start | bytes 3145732 | tf_op jit(solution)/shard_map/while
  644.2 12.9 %copy-start.10 = (bf16[1024,8,64]{0,2,1:T(8,128)(2,1)S(1)}, bf16[1024,8,64]{0,2,1:T(8,128)(2,1)}, u32[]{:S(2)}) copy-start(bf16[1024,8,64]{0,2,1:T(8,128)(2,1)} %copy-done.9) | copy-start | bytes 3145732 | tf_op jit(solution)/shard_map/while
  714.3 11.5 copy-start.11
  714.3 11.5 copy-start.17
  725.9 14.7 %copy-start = (bf16[8,512,1024]{2,1,0:T(8,128)(2,1)}, bf16[8,512,1024]{2,1,0:T(8,128)(2,1)S(1)}, u32[]{:S(2)}) copy-start(bf16[8,512,1024]{2,1,0:T(8,128)(2,1)S(1)} %multiply_convert_fusion.3) | copy-start | bytes 25165828 | tf_op jit(solution)/shard_map/while
  725.9 12.0 %copy-start.33 = (bf16[2,512,8,64]{1,3,2,0:T(8,128)(2,1)S(1)}, bf16[2,512,8,64]{1,3,2,0:T(8,128)(2,1)}, u32[]{:S(2)}) copy-start(bf16[2,512,8,64]{1,3,2,0:T(8,128)(2,1)} %get-tuple-element.751) | copy-start | bytes 3145732 | tf_op jit(solution)/shard_map/while
  744.4 12.2 %copy-start.5 = (f32[1024,8,64]{0,2,1:T(8,128)}, f32[1024,8,64]{0,2,1:T(8,128)S(1)}, u32[]{:S(2)}) copy-start(f32[1024,8,64]{0,2,1:T(8,128)S(1)} %bitcast_add_fusion.7) | copy-start | bytes 6291460 | tf_op jit(solution)/shard_map/while
  744.4 12.2 %copy-start.3 = (s32[524288]{0:T(1024)S(1)}, s32[524288]{0:T(1024)}, u32[]{:S(2)}) copy-start(s32[524288]{0:T(1024)} %copy-done.2) | copy-start | bytes 6291460 | tf_op jit(solution)/shard_map/while
  756.6 12.9 %copy-start.8 = (bf16[1024,8,64]{0,2,1:T(8,128)(2,1)S(1)}, bf16[1024,8,64]{0,2,1:T(8,128)(2,1)}, u32[]{:S(2)}) copy-start(bf16[1024,8,64]{0,2,1:T(8,128)(2,1)} %copy-done.7) | copy-start | bytes 3145732 | tf_op jit(solution)/shard_map/while
  756.6 12.9 %copy-start.10 = (bf16[1024,8,64]{0,2,1:T(8,128)(2,1)S(1)}, bf16[1024,8,64]{0,2,1:T(8,128)(2,1)}, u32[]{:S(2)}) copy-start(bf16[1024,8,64]{0,2,1:T(8,128)(2,1)} %copy-done.9) | copy-start | bytes 3145732 | tf_op jit(solution)/shard_map/while
  786.6 241.6 %reduce-scatter.11.cloned.1.call-start = ((), (), s32[]{:S(2)}) async-start(), calls=%async_computation.10 | async-start | bytes 4325376 | tf_op jit(solution)/shard_map/reduce_scatter | solution.py:255
  794.4 375.3 %reduce-scatter.9.cloned.1.call-start = ((), (), s32[]{:S(2)}) async-start(), calls=%async_computation.9 | async-start | bytes 4325376 | tf_op jit(solution)/shard_map/reduce_scatter | solution.py:253
  (61 other events, 169.4 us)
Sparse Core Ops, SparseCore 0:
  10.9 57.8 all-gather.3
  71.7 56.2 all-gather.5
  131.0 55.3 all-gather.7
  521.1 131.4 reduce-scatter.6
  786.7 97.5 reduce-scatter.4
  887.1 140.9 reduce-scatter.10
  1031.1 138.5 reduce-scatter.8
where the time goes:
time: 1180 us
  matrix products  413 us (35%)
  waiting for transfers between devices  302 us (26%)
  blocking collectives  155 us (13%)
  local copies, waits for them, and re-layouts  117 us (10%)
  other arithmetic  106 us (9%)
  loops' own time  68.9 us (6%)
  between operations  15 us (1%)
    reduce_scatter x1, waiting for transfers between devices, body(): lax.psum_scatter(reduce_w_grad, ('dp', 'fsdp'), scatter_dimension=0, tile...  144 us
    reduce_scatter x1, waiting for transfers between devices, body(): lax.psum_scatter(expand_w_grad, ('dp', 'fsdp'), scatter_dimension=0, tile...  142 us
    dot_general x6, matrix products, block_scores(): jnp.einsum('qhd,khd->hqk', block_q, key_heads, preferred_element_type=jnp...  135 us
    unnamed x2, blocking collectives  80.2 us
    dot_general x6, matrix products, block_scores(): jnp.dot(bias_table, onehot, preferred_element_type=jnp.float32)  77 us
    all_gather x1, blocking collectives, body(): lax.all_gather(output_weight, ('dp', 'fsdp'), axis=0, tiled=True)  75 us
    while x96, local copies, waits for them, and re-layouts  50.1 us
    dot_general x6, matrix products, inner_cols(): lax.dot_general(left_side, right_side, (((1,), (1,)), ((), ())), preferre...  47.7 us
  transfers between devices with their start and end apart: 7, of which 3 were waited for; matrix products, arithmetic and copies ran while one was open for 50% of the time, Pallas kernels for 0%

commit v1 on v0

v1 whole, which is shorter than its diff:
```python
import types

import jax
import jax.numpy as jnp
from jax import lax
from jax.experimental import pallas as pl
from jax.experimental.pallas import tpu as pltpu
from jax.sharding import PartitionSpec as P

D = 512
HEADS = 8
HEAD_DIM = 64
BUCKETS = 32
LONGEST = 512
TILE = 128
PAIRS = HEADS // 2
NEG = -1e30
eps = 1e-05
far_reach = 128

bf16 = jnp.bfloat16
f32 = jnp.float32
AXES = ("dp", "fsdp")


def iota(shape, dim):
    return lax.broadcasted_iota(jnp.int32, shape, dim)


def bucket_of(distance):
    exact_count = BUCKETS // 2
    counted = jnp.minimum(distance, exact_count)
    for level_j in range(1, exact_count):
        border = int(exact_count * (far_reach / exact_count) ** (level_j / exact_count))
        counted = counted + (distance >= border).astype(jnp.int32)
    return counted


def dot_nn(a, b):
    return lax.dot_general(a, b, (((1,), (0,)), ((), ())), preferred_element_type=f32)


def dot_nt(a, b):
    return lax.dot_general(a, b, (((1,), (1,)), ((), ())), preferred_element_type=f32)


def dot_tn(a, b):
    return lax.dot_general(a, b, (((0,), (0,)), ((), ())), preferred_element_type=f32)


def onehot(mask):
    return jnp.where(mask, 1.0, 0.0).astype(bf16)


def standardize(v):
    center = v - jnp.mean(v, axis=-1, keepdims=True)
    spread = jnp.mean(center * center, axis=-1, keepdims=True)
    rstd = lax.rsqrt(spread + eps)
    return center * rstd, rstd


def standardize_back(dx, xh, rstd):
    return rstd * (
        dx
        - jnp.mean(dx, axis=-1, keepdims=True)
        - xh * jnp.mean(dx * xh, axis=-1, keepdims=True)
    )


def gelu_parts(h):
    t = 1.0 / (1.0 + (0.3275911 * 0.7071067811865476) * jnp.abs(h))
    e = jnp.exp(-0.5 * h * h)
    poly = t * (
        0.127414796
        + t * (-0.142248368 + t * (0.7107068705 + t * (-0.7265760135 + t * 0.5307027145)))
    )
    tail = poly * e
    phi = jnp.where(h >= 0, 1.0 - tail, tail)
    return h * phi, phi + h * (e * 0.3989422804014327)


def split_heads(t):
    top = iota(t.shape, 0) < HEAD_DIM
    zero = jnp.zeros_like(t)
    return jnp.concatenate([jnp.where(top, t, zero), jnp.where(top, zero, t)], axis=1)


def join_heads(t):
    n = t.shape[1] // 2
    return jnp.concatenate([t[:HEAD_DIM, :n], t[HEAD_DIM:, n:]], axis=0)


def unpack_small(r, n):
    packed = r.A[:, 4 * D :]
    rows, lanes = iota((16 * n, D), 0), iota((16 * n, D), 1)
    per = D // n
    rep = onehot(iota((128, D), 1) % per == iota((128, D), 0))
    wide = dot_nn(packed, rep)
    wide = jnp.where(lanes // per == rows // 16, wide, 0.0)
    r.sm[...] = jnp.sum(wide.reshape(n, 16, D), axis=0)
    ff = r.es.shape[1]
    per = ff // n
    pick = onehot(iota((n, 16 * n), 1) == 16 * iota((n, 16 * n), 0) + 6)
    rep = onehot(iota((128, ff), 1) % per == iota((128, ff), 0))
    wide = dot_nn(dot_nn(pick, packed).astype(bf16), rep)
    wide = jnp.where(iota((n, ff), 1) // per == iota((n, ff), 0), wide, 0.0)
    r.es[...] = jnp.broadcast_to(jnp.sum(wide, axis=0, keepdims=True), r.es.shape)
    per = HEADS * BUCKETS // n
    group = BUCKETS // per
    pick = onehot(iota((n, 16 * n), 1) == 16 * iota((n, 16 * n), 0) + 7)
    bucket = bucket_of(iota((128, 256), 1))
    rep = onehot(bucket % per == iota((128, 256), 0))
    wide = dot_nn(dot_nn(pick, packed).astype(bf16), rep)
    bucket = bucket_of(iota((n, 256), 1))
    wide = jnp.where(bucket // per == iota((n, 256), 0) % group, wide, 0.0).astype(bf16)
    gather = onehot(iota((HEADS, n), 1) // group == iota((HEADS, n), 0))
    r.bd[...] = dot_nn(gather, wide)


def pack_small_grads(r, n):
    rows, lanes = iota((16 * n, D), 0), iota((16 * n, D), 1)
    per = D // n
    wide = jnp.broadcast_to(r.smg[...][None], (n, 16, D)).reshape(16 * n, D)
    wide = jnp.where(lanes // per == rows // 16, wide, 0.0).astype(bf16)
    rep = onehot(iota((128, D), 1) % per == iota((128, D), 0))
    packed = dot_nt(wide, rep)
    ff = r.esg.shape[1]
    per = ff // n
    rep = onehot(iota((128, ff), 1) % per == iota((128, ff), 0))
    wide = jnp.broadcast_to(r.esg[0:1, :], (n, ff))
    wide = jnp.where(iota((n, ff), 1) // per == iota((n, ff), 0), wide, 0.0).astype(bf16)
    part = dot_nt(wide, rep).astype(bf16)
    place = onehot(iota((16 * n, n), 0) == 16 * iota((16 * n, n), 1) + 6)
    packed = packed + dot_nn(place, part)
    per = HEADS * BUCKETS // n
    group = BUCKETS // per
    spread = onehot(iota((n, HEADS), 0) // group == iota((n, HEADS), 1))
    wide = dot_nn(spread, r.tg[...].astype(bf16))
    wide = jnp.where(iota((n, 128), 1) // per == iota((n, 128), 0) % group, wide, 0.0)
    rep = onehot(iota((128, 128), 1) % per == iota((128, 128), 0))
    part = dot_nt(wide.astype(bf16), rep).astype(bf16)
    place = onehot(iota((16 * n, n), 0) == 16 * iota((16 * n, n), 1) + 7)
    return packed + dot_nn(place, part)


def norm_first(r):
    def rows(i, c):
        s = pl.ds(pl.multiple_of(i * 256, 256), 256)
        xh, _ = standardize(r.x[s, :].astype(f32))
        r.na[s, :] = (xh * r.sm[0:1, :] + r.sm[1:2, :]).astype(bf16)
        return c

    lax.fori_loop(0, r.x.shape[0] // 256, rows, 0)


def masks(r):
    length = r.docs.shape[1]
    same = iota((128, length), 0) == r.docs[...]
    r.kd[...] = jnp.where(same, 1.0, 0.0).T.astype(bf16)
    differ = jnp.logical_and(iota((128, length), 0) < 8, jnp.logical_not(same))
    r.qd[...] = jnp.where(differ, NEG, 0.0).astype(bf16)


def near_bias(r):
    for h in range(HEADS):
        by_dist = r.bd[h : h + 1, :]
        by_dist = by_dist - by_dist[:, 255:256]
        line = jnp.concatenate([jnp.full((1, TILE), NEG, f32), by_dist], axis=1)
        line = jnp.broadcast_to(line, (TILE, 3 * TILE))
        line = pltpu.roll(line, 0, 1, stride=1, stride_axis=0)
        half = slice((h % 2) * TILE, (h % 2 + 1) * TILE)
        r.near[h // 2, 0:TILE, half] = line[:, 2 * TILE :]
        r.near[h // 2, TILE:, half] = line[:, TILE : 2 * TILE]


def project(r):
    def rows(i, c):
        s = pl.ds(pl.multiple_of(i * 256, 256), 256)
        out = dot_nn(r.na[s, :], r.A[:, 0 : 3 * D])
        q = (out[:, :D].astype(bf16) * bf16(HEAD_DIM**-0.5)).T
        k = out[:, D : 2 * D].astype(bf16)
        v = out[:, 2 * D :].astype(bf16)
        for p in range(PAIRS):
            lanes = slice(p * 128, (p + 1) * 128)
            r.qt[p, :, s] = q[lanes, :]
            r.k[p, s, :] = k[:, lanes]
            r.v[p, s, :] = v[:, lanes]
        return c

    lax.fori_loop(0, r.x.shape[0] // 256, rows, 0)


def bands(length):
    first = 0
    for b in range(length // TILE):
        low = max(0, b - LONGEST // TILE)
        count = (b + 1 - low) * TILE
        yield b, slice(low * TILE, (b + 1) * TILE), slice(b * TILE, (b + 1) * TILE), first, count
        first += count


def band_rows(length):
    return sum(count for _, _, _, _, count in bands(length))


def attend_forward(r, p):
    near = r.near[p]
    lanes = pl.ds(pl.multiple_of(p * 128, 128), 128)
    for b, ks, qs, first, count in bands(r.x.shape[0]):
        qd = r.qd[:, qs]
        rhs = jnp.concatenate(
            [split_heads(r.qt[p, :, qs]), jnp.concatenate([qd, qd], axis=1)], axis=0
        )
        lhs = jnp.concatenate([r.k[p, ks, :], r.kd[ks, :]], axis=1)
        st = dot_nn(lhs, rhs)
        if count > 2 * TILE:
            st = jnp.concatenate([st[: count - 2 * TILE], st[count - 2 * TILE :] + near], axis=0)
        else:
            st = st + near[2 * TILE - count :]
        lifted = jnp.exp(st - jnp.max(st, axis=0, keepdims=True))
        inverse = 1.0 / jnp.sum(lifted, axis=0, keepdims=True)
        weights = lifted.astype(bf16)
        r.P[p, first : first + count, :] = weights
        r.inv[p, b : b + 1, :] = inverse
        ot = join_heads(dot_tn(r.v[p, ks, :], weights) * inverse)
        r.ot[p, :, qs] = ot
        r.att[qs, lanes] = ot.T.astype(bf16)


def attend_backward(r, p):
    length = r.x.shape[0]
    r.dk[...] = jnp.zeros_like(r.dk)
    r.dv[...] = jnp.zeros_like(r.dv)
    r.acc[...] = jnp.zeros_like(r.acc)
    lanes = [pl.ds(pl.multiple_of(p * 128 + part * D, 128), 128) for part in range(3)]
    top = iota((128, TILE), 0) < HEAD_DIM
    for b, ks, qs, first, count in bands(length):
        inverse = r.inv[p, b : b + 1, :]
        scale = jnp.where(top, inverse[:, :TILE], inverse[:, TILE:])
        dot_ = (r.dot[p, :, qs] * scale).astype(bf16)
        prod = dot_.astype(f32) * r.ot[p, :, qs]
        delta = jnp.concatenate(
            [
                jnp.sum(prod[:HEAD_DIM], axis=0, keepdims=True),
                jnp.sum(prod[HEAD_DIM:], axis=0, keepdims=True),
            ],
            axis=1,
        )
        dcat = split_heads(dot_)
        weights = r.P[p, first : first + count, :]
        ds = weights.astype(f32) * (dot_nn(r.v[p, ks, :], dcat) - delta)
        dsb = ds.astype(bf16)
        if count >= 2 * TILE:
            r.acc[...] += ds[count - 2 * TILE :]
        else:
            r.acc[TILE:, :] += ds
        r.dv[ks, :] += dot_nt(weights, dcat)
        r.dk[ks, :] += dot_nt(dsb, split_heads(r.qt[p, :, qs]))
        dqt = join_heads(dot_tn(r.k[p, ks, :], dsb)) * HEAD_DIM**-0.5
        r.dproj[qs, lanes[0]] = dqt.T.astype(bf16)
    r.dproj[:, lanes[1]] = r.dk[...].astype(bf16)
    r.dproj[:, lanes[2]] = r.dv[...].astype(bf16)
    zero = jnp.zeros((TILE, TILE), f32)
    rows = iota((TILE, 3 * TILE), 0)
    for h in range(2):
        half = slice(h * TILE, (h + 1) * TILE)
        line = jnp.concatenate([zero, r.acc[TILE:, half], r.acc[:TILE, half]], axis=1)
        for bit in range(7):
            rolled = pltpu.roll(line, 3 * TILE - (1 << bit), 1)
            line = jnp.where((rows >> bit) & 1 == 1, rolled, line)
        r.lines[pl.ds(2 * p + h, 1), :] = jnp.sum(line, axis=0, keepdims=True)


def table_grad(r):
    by_dist = r.lines[:, TILE:]
    dist = iota((2 * TILE, 128), 0)
    near = jnp.logical_and(bucket_of(dist) == iota((2 * TILE, 128), 1), dist < 2 * TILE)
    near = jnp.logical_and(near, iota((2 * TILE, 128), 1) < BUCKETS - 1)
    counted = lax.dot_general(
        by_dist,
        jnp.where(near, 1.0, 0.0),
        (((1,), (0,)), ((), ())),
        precision=lax.Precision.HIGHEST,
        preferred_element_type=f32,
    )
    rest = -jnp.sum(counted, axis=1, keepdims=True)
    r.tg[...] = jnp.where(iota((HEADS, 128), 1) == BUCKETS - 1, rest, counted)


def middle(r):
    ff = r.es.shape[1]
    wide = 512
    r.smg[...] = jnp.zeros_like(r.smg)
    r.esg[...] = jnp.zeros_like(r.esg)

    def rows(i, c):
        s = pl.ds(pl.multiple_of(i * 256, 256), 256)
        residual = (
            r.x[s, :].astype(f32) + dot_nn(r.att[s, :], r.A[:, 3 * D : 4 * D]) + r.sm[2:3, :]
        )
        xh, rstd = standardize(residual)
        nf = (xh * r.sm[3:4, :] + r.sm[4:5, :]).astype(bf16)
        r.nf[s, :] = nf
        g = r.g[s, :]
        branch = jnp.zeros((256, D), f32)
        gnf = jnp.zeros((256, D), f32)
        for f in range(ff // wide):
            cols = slice(f * wide, (f + 1) * wide)
            hidden = dot_nn(nf, r.W1[:, cols]) + r.es[0:1, cols]
            active, slope = gelu_parts(hidden)
            active = active.astype(bf16)
            r.act[s, cols] = active
            gh = dot_nt(g, r.W2[cols, :]) * slope
            r.esg[0:1, cols] += jnp.sum(gh, axis=0, keepdims=True)
            gh = gh.astype(bf16)
            r.gh[s, cols] = gh
            branch = branch + dot_nn(active, r.W2[cols, :])
            gnf = gnf + dot_nt(gh, r.W1[:, cols])
        r.out[s, :] = (residual + branch + r.sm[5:6, :]).astype(bf16)
        gf = g.astype(f32)
        grad = gf + standardize_back(gnf * r.sm[3:4, :], xh, rstd)
        r.gres[s, :] = grad
        gb = grad.astype(bf16)
        r.gb[s, :] = gb
        r.smg[2:3, :] += jnp.sum(gb.astype(f32), axis=0, keepdims=True)
        r.smg[3:4, :] += jnp.sum(gnf * xh, axis=0, keepdims=True)
        r.smg[4:5, :] += jnp.sum(gnf, axis=0, keepdims=True)
        r.smg[5:6, :] += jnp.sum(gf, axis=0, keepdims=True)
        dot_ = dot_nt(gb, r.A[:, 3 * D : 4 * D]).T
        for p in range(PAIRS):
            r.dot[p, :, s] = dot_[p * 128 : (p + 1) * 128, :]
        return c

    lax.fori_loop(0, r.x.shape[0] // 256, rows, 0)


def last(r):
    def rows(i, c):
        s = pl.ds(pl.multiple_of(i * 256, 256), 256)
        gna = dot_nt(r.dproj[s, :], r.A[:, 0 : 3 * D])
        xh, rstd = standardize(r.x[s, :].astype(f32))
        r.igrad[s, :] = r.gres[s, :] + standardize_back(gna * r.sm[0:1, :], xh, rstd)
        r.smg[0:1, :] += jnp.sum(gna * xh, axis=0, keepdims=True)
        r.smg[1:2, :] += jnp.sum(gna, axis=0, keepdims=True)
        return c

    lax.fori_loop(0, r.x.shape[0] // 256, rows, 0)


def weight_grad(left, right, step, put):
    def rows(i, c):
        put(i, dot_tn(left[:, pl.ds(pl.multiple_of(i * step, step), step)], right[...]))
        return c

    lax.fori_loop(0, left.shape[1] // step, rows, 0)


class Place:
    def __init__(self, dp_size, fsdp_size):
        dp, x = lax.axis_index("dp"), lax.axis_index("fsdp")
        self.z, self.y, self.c, self.x = dp // 4, (dp // 2) % 2, dp % 2, x
        self.zs = dp_size // 4

    def zpeer(self, m):
        z = self.z
        return (z, z + 1 - 2 * (z % 2), (z + 2) % 4, 3 - z)[m]

    def index(self, m, t, other=False):
        x = 1 - self.x if t in (1, 3) else self.x
        y = 1 - self.y if t in (2, 3) else self.y
        c = 1 - self.c if other else self.c
        return ((self.zpeer(m) * 2 + y) * 2 + c) * 2 + x

    def inner(self, t, other=False):
        x = 1 - self.x if t in (1, 3) else self.x
        y = 1 - self.y if t in (2, 3) else self.y
        c = 1 - self.c if other else self.c
        return (y * 2 + c) * 2 + x

    def device(self, m=0, t=0, other=False):
        x = 1 - self.x if t in (1, 3) else self.x
        y = 1 - self.y if t in (2, 3) else self.y
        c = 1 - self.c if other else self.c
        return ((self.zpeer(m) * 2 + y) * 2 + c, x)

    def neighbours(self):
        return [self.device(m=m) for m in (1, 2, 3)] + [
            self.device(t=1),
            self.device(t=2),
            self.device(other=True),
        ]


def enter(place):
    barrier = pltpu.get_barrier_semaphore()
    for peer in place.neighbours():
        pl.semaphore_signal(
            barrier, inc=1, device_id=peer, device_id_type=pl.DeviceIdType.MESH
        )
    pl.semaphore_wait(barrier, 6)


GATHER_SEMS = 35
Z0, X0, Y0, OA0, OB0, S0 = -1, 3, 7, 11, 15, 19


class Gather:
    def __init__(self, place, whole, rho, half, send, recv):
        self.place, self.whole, self.rho, self.half = place, whole, rho, half
        self.send, self.recv = send, recv
        self.started = []

    def view(self, shard, part=None):
        rows = pl.ds(pl.multiple_of(shard * self.rho, 16), self.rho)
        if part is None:
            return self.whole.at[rows, :]
        cols = slice(0, self.half) if part == 0 else slice(self.half, self.whole.shape[1])
        return self.whole.at[rows, cols]

    def copy(self, shard, sem, device, part=None):
        ref = self.view(shard, part)
        return pltpu.make_async_remote_copy(
            src_ref=ref,
            dst_ref=ref,
            send_sem=self.send.at[sem],
            recv_sem=self.recv.at[sem],
            device_id=device,
            device_id_type=pl.DeviceIdType.MESH,
        )

    def start(self, shard, sem, device, part=None):
        self.copy(shard, sem, device, part).start()
        self.started.append((sem, part))

    def arrive(self, shard, sem, part=None):
        self.copy(shard, sem, self.place.device(other=True), part).wait_recv()

    def spread(self, m):
        at = self.place
        shard = at.index(m, 0)
        self.start(shard, X0 + m, at.device(t=1))
        self.start(shard, Y0 + m, at.device(t=2))
        self.start(shard, S0 + m, at.device(other=True))

    def first(self):
        at = self.place
        for m in (1, 2, 3):
            self.start(at.index(0, 0), Z0 + m, at.device(m=m))
        self.spread(0)

    def second(self, m):
        self.arrive(self.place.index(m, 0), Z0 + m)
        self.spread(m)

    def third(self, m):
        at = self.place
        shard = at.index(m, 1)
        self.arrive(shard, X0 + m)
        self.start(shard, OA0 + m, at.device(t=2), 0)
        self.start(shard, S0 + 4 + m, at.device(other=True))
        shard = at.index(m, 2)
        self.arrive(shard, Y0 + m)
        self.start(shard, OB0 + m, at.device(t=1), 1)
        self.start(shard, S0 + 8 + m, at.device(other=True))

    def fourth(self, m):
        at = self.place
        shard = at.index(m, 3)
        self.arrive(shard, OA0 + m, 0)
        self.arrive(shard, OB0 + m, 1)
        self.start(shard, S0 + 12 + m, at.device(other=True))

    def finish(self):
        for t in range(4):
            for m in range(4):
                self.arrive(self.place.index(m, t, other=True), S0 + 4 * t + m)

    def drain(self):
        at = self.place
        for sem, part in self.started:
            self.copy(at.index(0, 0), sem, at.device(other=True), part).wait_send()


SCATTER_SEMS = 11


class Scatter:
    def __init__(self, place, full, bufs, out, half, send, recv):
        self.place, self.full, self.out, self.half = place, full, out, half
        self.sib, self.ra, self.rb, self.rx, self.ry, self.rz = bufs
        self.send, self.recv = send, recv
        self.started = []

    def copy(self, src, dst, sem, device):
        return pltpu.make_async_remote_copy(
            src_ref=src,
            dst_ref=dst,
            send_sem=self.send.at[sem],
            recv_sem=self.recv.at[sem],
            device_id=device,
            device_id_type=pl.DeviceIdType.MESH,
        )

    def start(self, src, dst, sem, device):
        self.copy(src, dst, sem, device).start()
        self.started.append(sem)

    def arrive(self, dst, sem):
        self.copy(dst, dst, sem, self.place.device(other=True)).wait_recv()

    def first(self):
        at = self.place
        for t in (3, 1, 2, 0):
            self.start(
                self.full.at[:, at.inner(t, other=True)], self.sib.at[t], t, at.device(other=True)
            )

    def merge(self, t):
        self.arrive(self.sib.at[t], t)
        self.sib[t] += self.full[:, self.place.inner(t)]

    def second(self):
        at = self.place
        self.merge(3)
        self.start(self.sib.at[3, :, :, : self.half], self.ra, 4, at.device(t=1))
        self.start(self.sib.at[3, :, :, self.half :], self.rb, 5, at.device(t=2))

    def third(self):
        at = self.place
        self.merge(1)
        self.merge(2)
        self.arrive(self.rb, 5)
        self.sib[1, :, :, self.half :] += self.rb[...]
        self.start(self.sib.at[1], self.rx, 6, at.device(t=1))
        self.arrive(self.ra, 4)
        self.sib[2, :, :, : self.half] += self.ra[...]
        self.start(self.sib.at[2], self.ry, 7, at.device(t=2))

    def fourth(self):
        at = self.place
        self.merge(0)
        self.arrive(self.rx, 6)
        self.arrive(self.ry, 7)
        self.sib[0] += (self.rx[...].astype(f32) + self.ry[...].astype(f32)).astype(bf16)
        for m in (1, 2, 3):
            self.start(self.sib.at[0, at.zpeer(m)], self.rz.at[m - 1], 7 + m, at.device(m=m))

    def fifth(self):
        total = self.sib[0, self.place.z].astype(f32)
        for m in (1, 2, 3):
            self.arrive(self.rz.at[m - 1], 7 + m)
            total = total + self.rz[m - 1].astype(f32)
        self.out[...] = total

    def drain(self):
        for sem in self.started:
            if sem < 4:
                dst = self.sib.at[sem]
            elif sem < 8:
                dst = (self.ra, self.rb, self.rx, self.ry)[sem - 4]
            else:
                dst = self.rz.at[sem - 8]
            self.copy(dst, dst, sem, self.place.device(other=True)).wait_send()


def scatter_bufs(rho, cols, half):
    return [
        pltpu.VMEM((4, 4, rho, cols), bf16),
        pltpu.VMEM((4, rho, half), bf16),
        pltpu.VMEM((4, rho, cols - half), bf16),
        pltpu.VMEM((4, rho, cols), bf16),
        pltpu.VMEM((4, rho, cols), bf16),
        pltpu.VMEM((3, rho, cols), bf16),
    ]


def work_scratch(length, ff):
    tokens = band_rows(length)
    return dict(
        na=pltpu.VMEM((length, D), bf16),
        kd=pltpu.VMEM((length, 128), bf16),
        qd=pltpu.VMEM((128, length), bf16),
        near=pltpu.VMEM((PAIRS, 2 * TILE, 2 * TILE), f32),
        qt=pltpu.VMEM((PAIRS, 128, length), bf16),
        k=pltpu.VMEM((PAIRS, length, 128), bf16),
        v=pltpu.VMEM((PAIRS, length, 128), bf16),
        P=pltpu.VMEM((PAIRS, tokens, 2 * TILE), bf16),
        inv=pltpu.VMEM((PAIRS, length // TILE, 2 * TILE), f32),
        ot=pltpu.VMEM((PAIRS, 128, length), f32),
        att=pltpu.VMEM((length, D), bf16),
        nf=pltpu.VMEM((length, D), bf16),
        act=pltpu.VMEM((length, ff), bf16),
        gh=pltpu.VMEM((length, ff), bf16),
        gres=pltpu.VMEM((length, D), f32),
        gb=pltpu.VMEM((length, D), bf16),
        dot=pltpu.VMEM((PAIRS, 128, length), f32),
        dk=pltpu.VMEM((length, 128), f32),
        dv=pltpu.VMEM((length, 128), f32),
        acc=pltpu.VMEM((2 * TILE, 2 * TILE), f32),
        lines=pltpu.VMEM((HEADS, 3 * TILE), f32),
        dproj=pltpu.VMEM((length, 3 * D), bf16),
    )


def small_scratch(ff):
    return dict(
        sm=pltpu.VMEM((16, D), f32),
        es=pltpu.VMEM((8, ff), f32),
        bd=pltpu.VMEM((HEADS, 256), f32),
        smg=pltpu.VMEM((16, D), f32),
        esg=pltpu.VMEM((8, ff), f32),
        tg=pltpu.VMEM((HEADS, 128), f32),
    )


PARAMS = dict(vmem_limit_bytes=62 * 1024 * 1024)


def run_kernel(kernel, operands, out_shape, scratch, **params):
    names = list(scratch)
    count = len(operands) + len(out_shape)

    def named(*refs):
        kernel(refs[: len(operands)], refs[len(operands) : count], dict(zip(names, refs[count:])))

    return pl.pallas_call(
        named,
        out_shape=out_shape,
        in_specs=[pl.BlockSpec(memory_space=pltpu.VMEM)] * len(operands),
        out_specs=[pl.BlockSpec(memory_space=pltpu.VMEM)] * len(out_shape),
        scratch_shapes=[scratch[name] for name in names],
        compiler_params=pltpu.CompilerParams(**PARAMS, **params),
    )(*operands)


def whole_layer(x, documents, g, packed, w_a, w_o, w_1, w_2, dp_size, fsdp_size):
    n = dp_size * fsdp_size
    length, ff = x.shape[0], w_1.shape[1]
    ra, r2 = w_1.shape[0], w_2.shape[0]
    cols_a = 4 * D + 128
    work = work_scratch(length, ff)
    small = small_scratch(ff)
    scratch = dict(work, **small)
    scratch.update(
        A=pltpu.VMEM((n * ra, cols_a), bf16),
        W1=pltpu.VMEM((n * ra, ff), bf16),
        W2=pltpu.VMEM((n * r2, D), bf16),
        dA=pltpu.VMEM((4, 8, ra, cols_a), bf16),
        d1=pltpu.VMEM((4, 8, ra, ff), bf16),
        d2=pltpu.VMEM((4, 8, r2, D), bf16),
        gsend=pltpu.SemaphoreType.DMA((3, GATHER_SEMS)),
        grecv=pltpu.SemaphoreType.DMA((3, GATHER_SEMS)),
        ssend=pltpu.SemaphoreType.DMA((3, SCATTER_SEMS)),
        srecv=pltpu.SemaphoreType.DMA((3, SCATTER_SEMS)),
    )
    shapes = [(ra, cols_a, 1024), (ra, ff, ff // 2), (r2, D, D // 2)]
    for i, (rho, cols, half) in enumerate(shapes):
        for j, buf in enumerate(scatter_bufs(rho, cols, half)):
            scratch["buf%d_%d" % (i, j)] = buf

    def kernel(ins, outs, s):
        r = types.SimpleNamespace(**s)
        r.x, r.docs, r.g, own_small, own_a, own_o, own_1, own_2 = ins
        r.out, r.igrad, out_a, out_1, out_2 = outs
        at = Place(dp_size, fsdp_size)
        mine = at.index(0, 0)
        rows_a = pl.ds(pl.multiple_of(mine * ra, 16), ra)
        rows_2 = pl.ds(pl.multiple_of(mine * r2, 16), r2)
        r.A[rows_a, 0 : 3 * D] = own_a[...]
        r.A[rows_a, 3 * D : 4 * D] = own_o[...]
        r.A[rows_a, 4 * D :] = own_small[...]
        r.W1[rows_a, :] = own_1[...]
        r.W2[rows_2, :] = own_2[...]
        enter(at)
        gathers = [
            Gather(at, ref, rho, half, r.gsend.at[i], r.grecv.at[i])
            for i, (ref, (rho, _, half)) in enumerate(zip((r.A, r.W1, r.W2), shapes))
        ]
        ga, g1, g2 = gathers
        ga.first()
        masks(r)
        for m in (1, 2, 3):
            ga.second(m)
        for m in range(4):
            ga.third(m)
        g1.first()
        g2.first()
        for m in range(4):
            ga.fourth(m)
        ga.finish()
        unpack_small(r, n)
        near_bias(r)
        norm_first(r)
        project(r)

        def forward(p, c):
            attend_forward(r, p)

            @pl.when(p == 0)
            def _():
                for item in (g1, g2):
                    for m in (1, 2, 3):
                        item.second(m)

            @pl.when(p == 1)
            def _():
                for item in (g1, g2):
                    for m in range(4):
                        item.third(m)

            @pl.when(p == 2)
            def _():
                for item in (g1, g2):
                    for m in range(4):
                        item.fourth(m)

            return c

        lax.fori_loop(0, PAIRS, forward, 0)
        g1.finish()
        g2.finish()
        middle(r)

        def put_2(i, value):
            r.d2[i] = value.astype(bf16).reshape(8, r2, D)

        def put_1(i, value):
            r.d1[pl.ds(2 * i, 2)] = value.astype(bf16).reshape(2, 8, ra, ff)

        def put_o(i, value):
            r.dA[pl.ds(2 * i, 2), :, :, 3 * D : 4 * D] = value.astype(bf16).reshape(2, 8, ra, D)

        def put_a(i, value):
            r.dA[pl.ds(2 * i, 2), :, :, 0 : 3 * D] = value.astype(bf16).reshape(2, 8, ra, 3 * D)

        scatters = [
            Scatter(
                at,
                full,
                [s["buf%d_%d" % (i, j)] for j in range(6)],
                out,
                half,
                r.ssend.at[i],
                r.srecv.at[i],
            )
            for i, (full, out, (_, _, half)) in enumerate(
                zip((r.dA, r.d1, r.d2), (out_a, out_1, out_2), shapes)
            )
        ]
        sa, s1, s2 = scatters
        weight_grad(r.act, r.g, 512, put_2)
        s2.first()
        weight_grad(r.nf, r.gh, 256, put_1)
        s1.first()
        s2.second()
        weight_grad(r.att, r.gb, 256, put_o)

        def backward(p, c):
            attend_backward(r, p)

            @pl.when(p == 0)
            def _():
                s2.third()
                s1.second()

            @pl.when(p == 1)
            def _():
                s2.fourth()
                s1.third()

            @pl.when(p == 2)
            def _():
                s2.fifth()
                s1.fourth()

            return c

        lax.fori_loop(0, PAIRS, backward, 0)
        s1.fifth()
        table_grad(r)
        weight_grad(r.na, r.dproj, 256, put_a)
        last(r)
        tail = pack_small_grads(r, n).astype(bf16)
        r.dA[:, :, :, 4 * D :] = tail.reshape(4, 8, ra, 128)
        sa.first()
        sa.second()
        sa.third()
        sa.fourth()
        sa.fifth()
        for item in gathers + scatters:
            item.drain()

    out_shape = [
        jax.ShapeDtypeStruct((length, D), bf16),
        jax.ShapeDtypeStruct((length, D), f32),
        jax.ShapeDtypeStruct((ra, cols_a), f32),
        jax.ShapeDtypeStruct((ra, ff), f32),
        jax.ShapeDtypeStruct((r2, D), f32),
    ]
    operands = [x, documents, g, packed, w_a, w_o, w_1, w_2]
    return run_kernel(
        kernel, operands, out_shape, scratch, collective_id=0, has_side_effects=True
    )


def local_layer(x, documents, g, w_ao, w_1, w_2, sm, es, bd):
    length, ff = x.shape[0], w_1.shape[1]
    scratch = dict(work_scratch(length, ff))

    def kernel(ins, outs, s):
        r = types.SimpleNamespace(**s)
        r.x, r.docs, r.g, r.A, r.W1, r.W2, r.sm, r.es, r.bd = ins
        r.out, r.igrad, d_a, d_1, d_2, r.smg, r.esg, r.tg = outs
        masks(r)
        near_bias(r)
        norm_first(r)
        project(r)

        def forward(p, c):
            attend_forward(r, p)
            return c

        lax.fori_loop(0, PAIRS, forward, 0)
        middle(r)

        def put_into(ref, step, cols):
            def put(i, value):
                rows = pl.ds(pl.multiple_of(i * step, step), step)
                ref[rows, cols] = value.astype(ref.dtype)

            return put

        weight_grad(r.act, r.g, 512, put_into(d_2, 512, slice(None)))
        weight_grad(r.nf, r.gh, 256, put_into(d_1, 256, slice(None)))
        weight_grad(r.att, r.gb, 256, put_into(d_a, 256, slice(3 * D, 4 * D)))

        def backward(p, c):
            attend_backward(r, p)
            return c

        lax.fori_loop(0, PAIRS, backward, 0)
        table_grad(r)
        weight_grad(r.na, r.dproj, 256, put_into(d_a, 256, slice(0, 3 * D)))
        last(r)

    out_shape = [
        jax.ShapeDtypeStruct((length, D), bf16),
        jax.ShapeDtypeStruct((length, D), f32),
        jax.ShapeDtypeStruct((D, 4 * D), bf16),
        jax.ShapeDtypeStruct((D, ff), bf16),
        jax.ShapeDtypeStruct((ff, D), bf16),
        jax.ShapeDtypeStruct((16, D), f32),
        jax.ShapeDtypeStruct((8, ff), f32),
        jax.ShapeDtypeStruct((HEADS, 128), f32),
    ]
    return run_kernel(kernel, [x, documents, g, w_ao, w_1, w_2, sm, es, bd], out_shape, scratch)


def whole_body(dp_size, fsdp_size):
    def body(x, documents, fg, fs, w_a, table, w_o, os, sg, ss, w_1, es, w_2, rs, g):
        def row(v):
            return jnp.pad(v, (0, 128 - v.shape[0]))

        rows = [row(v) for v in (fg, fs, os, sg, ss, rs, es, table)]
        packed = jnp.concatenate([jnp.stack(rows), jnp.zeros((8, 128), bf16)], axis=0)
        out, igrad, d_a, d_1, d_2 = whole_layer(
            x, documents, g, packed, w_a, w_o, w_1, w_2, dp_size, fsdp_size
        )
        small = d_a[:, 4 * D :]

        def part(i, like):
            return small[i, : like.shape[0]]

        return (
            out,
            igrad,
            part(0, fg),
            part(1, fs),
            d_a[:, : 3 * D],
            part(7, table),
            d_a[:, 3 * D : 4 * D],
            part(2, os),
            part(3, sg),
            part(4, ss),
            d_1,
            part(6, es),
            d_2,
            part(5, rs),
        )

    return body


def split_body(x, documents, fg, fs, w_a, table, w_o, os, sg, ss, w_1, es, w_2, rs, g):
    def whole(v):
        return lax.all_gather(v, AXES, axis=0, tiled=True)

    def mine(v):
        return lax.psum_scatter(v.astype(f32), AXES, scatter_dimension=0, tiled=True)

    w_ao = whole(jnp.concatenate([w_a, w_o], axis=1))
    rows = [whole(v).astype(f32) for v in (fg, fs, os, sg, ss, rs)]
    sm = jnp.concatenate([jnp.stack(rows), jnp.zeros((10, D), f32)], axis=0)
    wide = whole(es).astype(f32)
    bias = whole(table).astype(f32).reshape(HEADS, BUCKETS)
    bd = bias[:, bucket_of(jnp.arange(256, dtype=jnp.int32))]
    out, igrad, d_a, d_1, d_2, smg, esg, tg = local_layer(
        x, documents, g, w_ao, whole(w_1), whole(w_2), sm, jnp.tile(wide[None], (8, 1)), bd
    )
    d_a = mine(d_a)
    return (
        out,
        igrad,
        mine(smg[0]),
        mine(smg[1]),
        d_a[:, : 3 * D],
        mine(tg[:, :BUCKETS].reshape(HEADS * BUCKETS)),
        d_a[:, 3 * D :],
        mine(smg[2]),
        mine(smg[3]),
        mine(smg[4]),
        mine(d_1),
        mine(esg[0]),
        mine(d_2),
        mine(smg[5]),
    )


def solution(mesh):
    rows, flat = P(AXES, None), P(AXES)
    dp_size, fsdp_size = mesh.shape["dp"], mesh.shape["fsdp"]
    one_kernel = (dp_size, fsdp_size) == (16, 2)
    return jax.shard_map(
        whole_body(dp_size, fsdp_size) if one_kernel else split_body,
        mesh=mesh,
        in_specs=(
            rows,
            rows,
            flat,
            flat,
            rows,
            flat,
            rows,
            flat,
            flat,
            flat,
            rows,
            flat,
            rows,
            flat,
            rows,
        ),
        out_specs=(rows, rows, flat, flat, rows, flat, rows, flat, flat, flat, rows, flat, rows, flat),
        check_vma=False,
    )
```

time: 1180 us -> 152 us (0.13)
  matrix products: 413 us -> 0 us
  waiting for transfers between devices: 302 us -> 0 us
  blocking collectives: 155 us -> 0 us
  Pallas kernels: 0 us -> 135 us
  other arithmetic: 106 us -> 0 us
  local copies, waits for them, and re-layouts: 117 us -> 15.7 us
  loops' own time: 68.9 us -> 0 us
  between operations: 15 us -> 0.67 us
    dot_general x38 -> x0, matrix products: 413 us -> none  [the longest x6 135 us: block_scores(): jnp.einsum('qhd,khd->hqk', block_q, key_heads, preferred_element_type=jnp...]
    reduce_scatter x4 -> x0, waiting for transfers between devices: 300 us -> none  [the longest x1 144 us: body(): lax.psum_scatter(reduce_w_grad, ('dp', 'fsdp'), scatter_dimension=0, tile...]
    pallas_call x0 -> x1, Pallas kernels: none -> 135 us  [run_kernel(): pl.pallas_call(named, out_shape=out_shape, in_specs=[pl.BlockSpec(memory_...]
    unnamed x2 -> x0, blocking collectives: 80.2 us -> none
    all_gather x1 -> x0, blocking collectives: 75 us -> none  [body(): lax.all_gather(output_weight, ('dp', 'fsdp'), axis=0, tiled=True)]
    another operation x3 -> x0, loops' own time: 68.9 us -> none  [the longest x1 36.4 us: attention_backward(): lax.scan(one_block, (zeros_kv, zeros_kv, zeros_table), jnp.arange(block_c...]
    while x96 -> x0, local copies, waits for them, and re-layouts: 50.1 us -> none
    sub x2 -> x0, other arithmetic: 27.6 us -> none  [one_block(): lifted = jnp.exp(scores - row_peak)]
  transfers between devices with their start and end apart: 7 -> 0, of which waited for: 3 -> 0; matrix products, arithmetic and copies ran while one was open for 50% -> 0% of each run, Pallas kernels for 0% -> 0%
where the time goes in v1:
time: 152 us; the launch traced here: 151 us
  Pallas kernels  135 us (89%)
  local copies, waits for them, and re-layouts  15.7 us (10%)
    pallas_call x1, Pallas kernels, run_kernel(): pl.pallas_call(named, out_shape=out_shape, in_specs=[pl.BlockSpec(memory_...  135 us
    unnamed x10, local copies, waits for them, and re-layouts  4.9 us
    squeeze x3, local copies, waits for them, and re-layouts, part(): return small[i, :like.shape[0]]  3.96 us

profile of v1, /device:TPU:0, one launch (start us, length us, event | category | flops | bytes accessed | tf_op | source)
XLA Modules:
  0.0 151.1 jit_solution(2172205281893248294)
XLA Ops:
  0.6 0.7 pad_bitcast_fusion.6
  1.3 0.7 pad_bitcast_fusion
  2.0 0.7 pad_bitcast_fusion.4
  2.7 0.7 pad_bitcast_fusion.2
  3.4 1.2 concatenate.3.refs_3_
  4.5 134.8 %shard_map.254 = (bf16[1024,512]{1,0:T(8,128)(2,1)}, f32[1024,512]{1,0:T(8,128)}, f32[16,2176]{1,0:T(8,128)}, f32[16,2048]{1,0:T(8,128)}, f32[64,512]{1,0:T(8,128)}) custom-call(bf16[1024,512]{1,0:T(8,128)(2,1)} %refs_0_.1, s32[1,1024]{1,0:T(1,128)} %refs_1_.1, bf16[1024,512]{1,0:T(8,128)(2,1)} %refs_2_.1, bf16[16,128]{1,0:T(8,128)(2,1)} %concatenate.3.refs_3_, ...), custom_call_target="tpu_custom_call" | custom-call | tf_op jit(solution)/shard_map/pallas_call | solution.py:626
  139.3 0.0 copy-start
  139.3 1.3 slice_bitcast_fusion.5
  140.7 1.2 slice_bitcast_fusion.1
  141.9 1.4 slice_bitcast_fusion
  143.3 1.4 slice.43
  144.7 1.5 %slice.41 = f32[16,1536]{1,0:T(8,128)} slice(f32[16,2176]{1,0:T(8,128)} %get-tuple-element.21), slice={[0:16], [0:1536]} | slice | bytes 196608 | tf_op jit(solution)/shard_map/slice | solution.py:879
  146.2 2.3 %copy.33 = bf16[1024,512]{1,0:T(8,128)(2,1)} copy(bf16[1024,512]{1,0:T(8,128)(2,1)} %get-tuple-element.52) | data formatting | bytes 2097152
  148.5 0.0 copy-done
  148.5 0.0 copy-start.2
  148.5 0.0 copy-start.1
  148.5 1.3 copy.34
  149.8 0.0 copy-done.2
  149.8 0.7 copy.35
  150.5 0.0 copy-done.1
  150.5 0.7 copy.36
  (1 shorter events, 0.0 us)
Async XLA Ops:
  139.3 9.2 %copy-start = (f32[1024,512]{1,0:T(8,128)S(1)}, f32[1024,512]{1,0:T(8,128)}, u32[]{:S(2)}) copy-start(f32[1024,512]{1,0:T(8,128)} %get-tuple-element.53) | copy-start | bytes 6291460
  148.5 1.3 copy-start.2
  148.5 2.0 %copy-start.1 = (f32[64,512]{1,0:T(8,128)S(1)}, f32[64,512]{1,0:T(8,128)}, u32[]{:S(2)}) copy-start(f32[64,512]{1,0:T(8,128)} %get-tuple-element.64) | copy-start | bytes 393220
